TPU v7x, 32 devices: a whole 2x2x4 slice. The times are simulated.
32 devices in a mesh: scen: 4 (over y, x), gx: 2 (over core), gy: 4 (over z).
Axes of the slice: x: 2, y: 2, z: 4, core: 2. Of those that a mesh axis runs over, the one named last changes fastest.
Arguments:
- perm_log: float32 [2, 128, 512], P(None, 'gx', 'gy'), may hold values from -2.5 to 2.5
- facies: int32 [2, 128, 512], P(None, 'gx', 'gy'), may hold values from 0 to 3
- facies_scale: float32 [4], replicated, may hold values from 0.5 to 2
- accumulation: float32 [2, 128, 512], P(None, 'gx', 'gy'), may hold values from 0.05 to 0.5
- previous_pressure: float32 [4, 2, 128, 512], P('scen', None, 'gx', 'gy'), may hold values from -6 to 6
- observed: float32 [4, 2, 128, 512], P('scen', None, 'gx', 'gy'), may hold values from -6 to 6
- well_cells: int32 [4, 5], P('scen'), may hold values from 0 to 131071
- well_rates: float32 [4, 5], P('scen'), may hold values from 5 to 20
Outputs:
- pressure: float32 [4, 2, 128, 512], P('scen', None, 'gx', 'gy')
- adjoint: float32 [4, 2, 128, 512], P('scen', None, 'gx', 'gy')
- gradient: float32 [2, 128, 512], P(None, 'gx', 'gy')
Inputs may be any that keep to these rules, and one draw needn't show every extreme that they name: `well_cells`: a flat index layer * 128 * 512 + row * 512 + column of a grid cell; several wells may share a cell.
All inputs are finite; a program needn't handle non-finite values.
Results may differ from a plain program's by a relative error of at most 0.0001.
Values sent between devices are 32-bit elements; how exact they have to be, the bound alone decides.
No kernel may reach another device: no remote copies, remote signals or barrier semaphores. Data moves between devices by JAX's collectives and lax.ppermute only.
A program may use at most 128 MiB of HBM per device.

v0:
```python
from functools import partial

import jax
import jax.numpy as jnp
from jax import lax
from jax.experimental import pallas as pl
from jax.experimental.pallas import tpu as pltpu
from jax.sharding import PartitionSpec as P

WELLS = 5
FACIES = 4
LAYERS = 2
SMOOTH = 2
COARSE = 4

vertical = 0.3
damping = 0.8

LANES = 128
HALF = 64
SUB = 8
PERM, ACC, PREV, OBS = range(4)
NEAR = 26
ROOM = HALF // 2 - NEAR
LEVELS = ((2, 1), (1, 1), (1, 2))


def lane_index():
    return lax.broadcasted_iota(jnp.int32, (SUB, LANES), 1)


def row_index():
    return lax.broadcasted_iota(jnp.int32, (SUB, LANES), 0)


def lane_roll(value, shift):
    return pltpu.roll(value, shift % LANES, value.ndim - 1)


def row_roll(value, shift):
    return pltpu.roll(value, shift % SUB, 0)


def shuffle(value, inverse):
    rows = lax.broadcasted_iota(jnp.int32, (LANES, LANES), 0)
    cols = lax.broadcasted_iota(jnp.int32, (LANES, LANES), 1)
    natural, place = (cols, rows) if inverse else (rows, cols)
    matrix = (natural == 2 * (place % HALF) + place // HALF).astype(jnp.bfloat16)
    rest = value.reshape(-1, LANES)
    total = None
    for _ in range(3):
        part = rest.astype(jnp.bfloat16)
        rest = rest - part.astype(jnp.float32)
        moved_part = jnp.dot(part, matrix, preferred_element_type=jnp.float32)
        total = moved_part if total is None else total + moved_part
    return total.reshape(value.shape)


def place_in_half(shape):
    return lax.broadcasted_iota(jnp.int32, shape, len(shape) - 1) % HALF


def spare_lanes(number, place):
    shift = NEAR - number * ROOM
    low, high = number * ROOM, HALF - (number + 1) * ROOM
    return (((place >= NEAR) & (place < HALF // 2), (place >= low) & (place < low + ROOM), shift),
            ((place >= HALF // 2) & (place < HALF - NEAR), (place >= high) & (place < high + ROOM), -shift))


def pack_kernel(scale_hbm, perm_log_hbm, facies_hbm, acc_hbm, prev_hbm, obs_hbm, own, message_a, message_b,
                scale, perm_log, facies, acc, prev, obs, sems):
    pairs = ((scale_hbm, scale), (perm_log_hbm, perm_log), (facies_hbm, facies), (acc_hbm, acc), (prev_hbm, prev),
             (obs_hbm, obs))
    copies = [pltpu.make_async_copy(source, target, sems.at[i]) for i, (source, target) in enumerate(pairs)]
    for copy in copies:
        copy.start()
    for copy in copies:
        copy.wait()
    label = facies[...]
    factor = jnp.zeros(label.shape, jnp.float32)
    for number in range(FACIES):
        factor = factor + jnp.where(label == number, scale[number], jnp.float32(0.0))
    fields = [shuffle(value, False) for value in (jnp.exp(perm_log[...]) * factor, acc[...], prev[0], obs[0])]
    for number in range(4):
        own[number] = fields[number]
    place = place_in_half(label.shape)
    full = []
    for number in range(3):
        value = fields[number]
        for lanes, _, shift in spare_lanes(number, place):
            value = jnp.where(lanes, lane_roll(fields[OBS], shift), value)
        full.append(value)
    low = place_in_half(label.shape[1:]) < HALF // 2
    left_first = low == (lax.axis_index("gy") % 2 == 1)
    couples = [(full[0][layer], full[1][layer]) for layer in range(LAYERS)] + [(full[2][0], full[2][1])]
    for plane, (one, two) in enumerate(couples):
        first, second = lane_roll(one, HALF), lane_roll(two, HALF + HALF // 2)
        message_a[plane] = jnp.where(left_first, first, second)
        message_b[plane] = jnp.where(left_first, second, first)


def merge_kernel(message_a, message_b, beside):
    place = place_in_half(beside.shape[2:])
    gy, gy_count = lax.axis_index("gy"), lax.axis_size("gy")
    inside = ((place < HALF // 2) & (gy < gy_count - 1)) | ((place >= HALF // 2) & (gy > 0))
    from_a = (place < HALF // 2) != (lax.axis_index("gy") % 2 == 1)
    full = [[], [], []]
    for plane in range(3):
        a, b = message_a[plane], message_b[plane]
        one = jnp.where(from_a, a, b)
        two = lane_roll(jnp.where(from_a, b, a), -(HALF // 2))
        for number, value in zip((0, 1) if plane < 2 else (2, 2), (one, two)):
            full[number].append(value)
    near = ((place < NEAR) | (place >= HALF - NEAR)) & inside
    for layer in range(LAYERS):
        observed = jnp.zeros(place.shape, jnp.float32)
        for number in range(3):
            value = full[number][layer]
            beside[number, layer] = jnp.where(near, value, 0.0)
            for _, lanes, shift in spare_lanes(number, place):
                observed = jnp.where(lanes, lane_roll(value, -shift), observed)
        beside[OBS, layer] = jnp.where(inside, observed, 0.0)


class Level:
    def __init__(self, count, width, span, blocks, refs):
        self.count = count
        self.width = width
        self.span = span
        self.blocks = blocks
        (self.c_south, self.c_first, self.c_inner, self.c_east, self.c_west, self.c_layer, self.weight, self.diag,
         self.target, self.now, self.later) = refs

    @staticmethod
    def scratch(count, width, blocks):
        def vectors(*lead):
            return pltpu.VMEM(lead + (SUB, LANES), jnp.float32)

        whole = vectors(LAYERS, width, blocks, count)
        edge = vectors(LAYERS, blocks, count)
        return [whole, vectors(LAYERS, width, blocks), edge, edge, edge, vectors(width, blocks, count)] + [whole] * 5

    def steps(self, ring=None):
        for b in range(self.blocks):
            for t in range(self.count):
                if ring is None or b == 0 or t < ring or t >= self.count - ring:
                    yield b, t

    def members(self):
        for layer in range(LAYERS):
            for u in range(self.width):
                yield layer, u


def row_before(values):
    edge = row_index() < 1
    rolled = [row_roll(value, 1) for value in values]
    return [jnp.where(edge, rolled[b - 1], rolled[b]) for b in range(len(values))]


def row_after(values):
    edge = row_index() >= SUB - 1
    rolled = [row_roll(value, -1) for value in values]
    return [jnp.where(edge, rolled[(b + 1) % len(values)], rolled[b]) for b in range(len(values))]


class Field:
    def __init__(self, level, source, coarse=None):
        self.source = source
        self.coarse = coarse
        self.count = level.count
        self.read = {}
        self.before, self.after = {}, {}
        for layer, u in level.members():
            lows = row_before([self.value(layer, u, b, level.count - 1) for b in range(level.blocks)])
            highs = row_after([self.value(layer, u, b, 0) for b in range(level.blocks)])
            for b in range(level.blocks):
                self.before[layer, u, b] = lows[b]
                self.after[layer, u, b] = highs[b]

    def value(self, layer, u, b, t):
        value = self.source[layer, u, b, t]
        return value if self.coarse is None else value + self.coarse[layer, 0, b, t // 2]

    def at(self, layer, u, b, t):
        if t < 0:
            return self.before[layer, u, b]
        if t >= self.count:
            return self.after[layer, u, b]
        key = layer, u, b, t
        if key not in self.read:
            self.read[key] = self.value(*key)
        return self.read[key]


def row_coeff(level, layer, u, b, t):
    return level.c_south[layer, u, b, t] if t >= 0 else level.c_first[layer, u, b]


def neighbour_sums(level, source, ring=None, coarse=None):
    field = Field(level, source, coarse)
    coeffs = {}
    for b, t in level.steps(ring):
        for member in level.members():
            for at in (t - 1, t):
                if (member, b, at) not in coeffs:
                    coeffs[member, b, at] = row_coeff(level, *member, b, at)
        layer_coeffs = [level.c_layer[u, b, t] for u in range(level.width)]
        for layer in range(LAYERS):
            here = [field.at(layer, u, b, t) for u in range(level.width)]
            east_coeff, west_coeff = level.c_east[layer, b, t], level.c_west[layer, b, t]
            if level.width == 2:
                inner = level.c_inner[layer, b, t]
                beside = [inner * here[1] + west_coeff * lane_roll(here[1], 1),
                          inner * here[0] + east_coeff * lane_roll(here[0], -1)]
            else:
                beside = [east_coeff * lane_roll(here[0], -level.span) + west_coeff * lane_roll(here[0], level.span)]
            for u in range(level.width):
                total = (coeffs[(layer, u), b, t - 1] * field.at(layer, u, b, t - 1)
                         + coeffs[(layer, u), b, t] * field.at(layer, u, b, t + 1)
                         + (beside[u] + layer_coeffs[u] * field.at(1 - layer, u, b, t)))
                yield (layer, u, b, t), here[u], total


def sweep(level, source, result, ring=None, coarse=None):
    for key, value, total in neighbour_sums(level, source, ring, coarse):
        result[key] = (1.0 - damping) * value + level.weight[key] * (level.target[key] + total)


def sweeps(level, count, ring=None, coarse=None):
    for number in range(count):
        sweep(level, level.now, level.later, None if ring is None else ring + count - 1 - number,
              coarse if number == 0 else None)
        level.now, level.later = level.later, level.now


def first_sweep(level):
    for b, t in level.steps():
        for layer, u in level.members():
            key = layer, u, b, t
            level.now[key] = level.weight[key] * level.target[key]


def pair_sum(value, span):
    lower = lane_index() % (2 * span) < span
    return value + jnp.where(lower, lane_roll(value, -span), lane_roll(value, span))


def low_group(value, span):
    return jnp.where(lane_index() % (2 * span) < span, value, lane_roll(value, span))


def high_group(value, span):
    return jnp.where(lane_index() % (2 * span) < span, lane_roll(value, -span), value)


def column_sum(values, level):
    return values[0] + values[1] if level.width == 2 else pair_sum(values[0], level.span)


def restrict_residual(fine, coarse):
    residuals = {}
    for key, value, total in neighbour_sums(fine, fine.now):
        layer, u, b, t = key
        residuals[key] = fine.target[key] + total - fine.diag[key] * value
        if t % 2 == 1 and u == fine.width - 1:
            rows = [residuals[layer, v, b, t - 1] + residuals[layer, v, b, t] for v in range(fine.width)]
            coarse.target[layer, 0, b, t // 2] = column_sum(rows, fine)


def vcycle(levels, from_zero, ring=None):
    finest, middle, bottom = levels
    if from_zero:
        first_sweep(finest)
    sweeps(finest, SMOOTH - int(from_zero))
    restrict_residual(finest, middle)
    first_sweep(middle)
    sweeps(middle, SMOOTH - 1)
    restrict_residual(middle, bottom)
    first_sweep(bottom)
    sweeps(bottom, COARSE - 1)
    sweeps(middle, SMOOTH, None, bottom.now)
    sweeps(finest, SMOOTH, ring, middle.now)


def harmonic(left, right):
    return 2.0 * left * right / jnp.maximum(left + right, 1e-20)


def finest_coeffs(level, perm, joined):
    last = level.count - 1
    for layer, u in level.members():
        heads = [perm[layer, u, b, 0] for b in range(level.blocks)]
        rolled = [row_roll(value, -1) for value in heads]
        edge = row_index() >= SUB - 1
        for b in range(level.blocks):
            after = jnp.where(edge, joined[b] * rolled[(b + 1) % level.blocks], rolled[b])
            for t in range(level.count):
                beyond = perm[layer, u, b, t + 1] if t < last else after
                level.c_south[layer, u, b, t] = harmonic(perm[layer, u, b, t], beyond)
        firsts = row_before([level.c_south[layer, u, b, last] for b in range(level.blocks)])
        for b in range(level.blocks):
            level.c_first[layer, u, b] = firsts[b]
    for b, t in level.steps():
        for u in range(level.width):
            level.c_layer[u, b, t] = vertical * harmonic(perm[0, u, b, t], perm[1, u, b, t])
        for layer in range(LAYERS):
            even, odd = perm[layer, 0, b, t], perm[layer, 1, b, t]
            level.c_inner[layer, b, t] = harmonic(even, odd)
            east = harmonic(odd, lane_roll(even, -1))
            level.c_east[layer, b, t] = east
            level.c_west[layer, b, t] = lane_roll(east, 1)


def with_weight(level, acc):
    for b, t in level.steps():
        for layer, u in level.members():
            key = layer, u, b, t
            if level.width == 2:
                beside = level.c_inner[layer, b, t] + (level.c_west, level.c_east)[u][layer, b, t]
            else:
                beside = level.c_west[layer, b, t] + level.c_east[layer, b, t]
            diag = (row_coeff(level, layer, u, b, t - 1) + row_coeff(level, layer, u, b, t)
                    + (beside + level.c_layer[u, b, t]) + acc[key])
            level.diag[key] = diag
            level.weight[key] = damping / jnp.maximum(diag, 1e-20)


def coarse_coeffs(fine, coarse, fine_acc, coarse_acc):
    width = range(fine.width)
    for b in range(coarse.blocks):
        for layer in range(LAYERS):
            coarse.c_first[layer, 0, b] = column_sum([fine.c_first[layer, u, b] for u in width], fine)
    for b, t in coarse.steps():
        one, two = 2 * t, 2 * t + 1
        coarse.c_layer[0, b, t] = column_sum([fine.c_layer[u, b, one] + fine.c_layer[u, b, two] for u in width], fine)
        for layer in range(LAYERS):
            coarse.c_south[layer, 0, b, t] = column_sum([fine.c_south[layer, u, b, two] for u in width], fine)
            coarse_acc[layer, 0, b, t] = column_sum(
                [fine_acc[layer, u, b, one] + fine_acc[layer, u, b, two] for u in width], fine)
            west = fine.c_west[layer, b, one] + fine.c_west[layer, b, two]
            east = fine.c_east[layer, b, one] + fine.c_east[layer, b, two]
            if fine.width == 1:
                west, east = low_group(west, fine.span), high_group(east, fine.span)
            coarse.c_west[layer, b, t] = west
            coarse.c_east[layer, b, t] = east
    with_weight(coarse, coarse_acc)


def own_columns(even, odd):
    return jnp.where(lane_index() < HALF, even, lane_roll(odd, HALF))


def face_terms(level, pressure, adjoint, perm):
    def face(coeff, one, two):
        changes = [field.at(*one) - (field.at(*two) if isinstance(two, tuple) else two[number])
                   for number, field in enumerate((pressure, adjoint))]
        return (coeff * coeff) * (changes[0] * changes[1])

    rows = {(layer, u): face(level.c_first[layer, u, 0], (layer, u, 0, -1), (layer, u, 0, 0))
            for layer, u in level.members()}
    for t in range(level.count):
        between = [(1.0 / vertical) * face(level.c_layer[u, 0, t], (0, u, 0, t), (1, u, 0, t)) for u in range(2)]
        for layer in range(LAYERS):
            inner = face(level.c_inner[layer, 0, t], (layer, 0, 0, t), (layer, 1, 0, t))
            easts = [lane_roll(field.at(layer, 0, 0, t), -1) for field in (pressure, adjoint)]
            east = face(level.c_east[layer, 0, t], (layer, 1, 0, t), easts)
            terms = []
            for u in range(2):
                south = face(level.c_south[layer, u, 0, t], (layer, u, 0, t), (layer, u, 0, t + 1))
                beside = lane_roll(east, 1) if u == 0 else east
                total = rows[layer, u] + south + (inner + beside) + between[u]
                rows[layer, u] = south
                terms.append(-0.5 * total / perm[layer, u, 0, t])
            yield layer, t, own_columns(*terms)


def order_kernel(shuffled, ordered):
    ordered[...] = shuffle(shuffled[...], True)


def cycle_kernel(grid_shape, blocks, *refs):
    cells_hbm, rates_hbm = refs[:2]
    inputs = [refs[2 + 2 * b:4 + 2 * b] for b in range(blocks)]
    refs = refs[2 + 2 * blocks:]
    pressure_out, adjoint_out, terms_out = refs[:3]
    cells, rates, sems, perm, acc, middle_acc, bottom_acc, pressure, pressure_rows, terms_rows = refs[3:13]
    refs = refs[13:]
    copies = [pltpu.make_async_copy(cells_hbm, cells, sems.at[0]), pltpu.make_async_copy(rates_hbm, rates, sems.at[1])]
    for copy in copies:
        copy.start()
    count = inputs[0][0].shape[2] // SUB
    levels = [Level(count >> depth, width, span, blocks, refs[11 * depth:11 * depth + 11])
              for depth, (width, span) in enumerate(LEVELS)]
    finest, middle, bottom = levels

    def rows(t):
        return pl.ds(t, SUB, stride=count)

    def fields(number, layer, b, t):
        low = lane_index() < HALF
        own, beside = [value[number, layer, rows(t), :] for value in inputs[b]]
        return jnp.where(low, own, beside), lane_roll(jnp.where(low, beside, own), HALF)

    gx = lax.axis_index("gx")
    if blocks == 3:
        joined = [1.0, 0.0, 1.0]
    elif blocks == 2:
        joined = [1.0 - gx.astype(jnp.float32), gx.astype(jnp.float32)]
    else:
        joined = [0.0]

    for b, t in finest.steps():
        for layer in range(LAYERS):
            perms, accs, starts = [fields(number, layer, b, t) for number in (PERM, ACC, PREV)]
            for u in range(2):
                key = layer, u, b, t
                perm[key] = perms[u]
                acc[key] = accs[u]
                finest.now[key] = starts[u]
                finest.target[key] = accs[u] * starts[u]

    for copy in copies:
        copy.wait()
    layer_count, total_rows, total_cols = grid_shape
    block_rows, block_cols = SUB * count, LANES
    for well in range(WELLS):
        cell = cells[0, well]
        layer = cell // (total_rows * total_cols)
        row = cell // total_cols % total_rows - gx * block_rows
        col = cell % total_cols - lax.axis_index("gy") * block_cols
        if blocks == 3:
            row_inside = (row >= -block_rows) & (row < 2 * block_rows)
        elif blocks == 2:
            row_inside = row >= -block_rows
        else:
            row_inside = row >= 0
        inside = row_inside & (col >= -HALF) & (col < block_cols + HALF)
        row = jnp.where(row < 0, row + blocks * block_rows, row)
        col = jnp.where(col < 0, col + 2 * block_cols, col)
        row = jnp.where(inside, row, 0)
        col = jnp.where(inside, col, 0)
        rate = jnp.where(inside, rates[0, well], 0.0)
        in_block = row % block_rows
        place = layer, col % 2, row // block_rows, in_block % count
        hit = (row_index() == in_block // count) & (lane_index() == col // 2)
        finest.target[place] = finest.target[place] + jnp.where(hit, rate, 0.0)

    finest_coeffs(finest, perm, joined)
    with_weight(finest, acc)
    coarse_coeffs(finest, middle, acc, middle_acc)
    coarse_coeffs(middle, bottom, middle_acc, bottom_acc)

    vcycle(levels, False)
    for b, t in finest.steps():
        for layer in range(LAYERS):
            observed = fields(OBS, layer, b, t)
            values = []
            for u in range(2):
                key = layer, u, b, t
                values.append(finest.now[key])
                pressure[key] = values[u]
                finest.target[key] = values[u] - observed[u]
            if b == 0:
                pressure_rows[0, layer, rows(t), :] = own_columns(*values)
    pressure_rows[...] = shuffle(pressure_rows[...], True)
    pressure_copy = pltpu.make_async_copy(pressure_rows, pressure_out, sems.at[2])
    pressure_copy.start()
    vcycle(levels, True, 1)
    for t in range(count):
        for layer in range(LAYERS):
            adjoint_out[0, layer, rows(t), :] = own_columns(*[finest.now[layer, u, 0, t] for u in range(2)])

    for layer, t, terms in face_terms(finest, Field(finest, pressure), Field(finest, finest.now), perm):
        terms_rows[layer, rows(t), :] = terms
    terms_out[...] = shuffle(terms_rows[...], True)
    pressure_copy.wait()


def moved(value, axis, step):
    count = lax.axis_size(axis)
    ring = axis == "gx" and count == 2
    pairs = [((i + step) % count, i) for i in range(count) if ring or 0 <= i + step < count]
    return lax.ppermute(value, axis, pairs)


def swapped(value, axis, first):
    count = lax.axis_size(axis)
    pairs = {i: i for i in range(count)}
    for i in range(first, count - 1, 2):
        pairs[i], pairs[i + 1] = i + 1, i
    return lax.ppermute(value, axis, list(pairs.items()))


def summed(value, axis):
    count = lax.axis_size(axis)
    others = [lax.ppermute(value, axis, [(i, i ^ step) for i in range(count)]) for step in range(count - 1, 0, -1)]
    terms = [value] + others[::-1]
    while len(terms) > 1:
        terms = [terms[i] + terms[i + 1] for i in range(0, len(terms), 2)]
    return terms[0]


def in_hbm(value):
    return pltpu.with_memory_space_constraint(value, pltpu.HBM)


def in_vmem(value):
    return pltpu.with_memory_space_constraint(value, pltpu.VMEM)


def shards(
    perm_log,
    facies,
    facies_scale,
    accumulation,
    previous_pressure,
    observed,
    well_cells,
    well_rates,
):
    layer_count, row_count, col_count = perm_log.shape
    gx_count, gy_count = lax.axis_size("gx"), lax.axis_size("gy")
    vmem = pl.BlockSpec(memory_space=pltpu.VMEM)
    hbm = pl.BlockSpec(memory_space=pltpu.HBM)
    f32 = jnp.float32
    fields = (perm_log, facies, accumulation, previous_pressure, observed)
    block = (layer_count, row_count, col_count)
    own, message_a, message_b = pl.pallas_call(
        pack_kernel,
        out_shape=[
            pltpu.VMEM((4,) + block, f32),
            pltpu.VMEM((3,) + block[1:], f32),
            pltpu.VMEM((3,) + block[1:], f32),
        ],
        in_specs=[hbm] * 6,
        out_specs=[vmem] * 3,
        scratch_shapes=[pltpu.SMEM(facies_scale.shape, f32)]
        + [pltpu.VMEM(value.shape, value.dtype) for value in fields] + [pltpu.SemaphoreType.DMA((6,))],
        name="pack",
    )(in_hbm(facies_scale), *[in_hbm(value) for value in fields])

    steps = (0, 1) if gx_count == 2 else (0, 1, -1) if gx_count > 2 else (0,)
    blocks = len(steps)
    owns = [own] + [moved(own, "gx", step) for step in steps[1:]]
    beside = pl.pallas_call(
        merge_kernel,
        out_shape=pltpu.VMEM((4, layer_count, row_count, col_count), f32),
        in_specs=[vmem] * 2,
        out_specs=vmem,
        name="merge",
    )(in_vmem(swapped(message_a, "gy", 0)), in_vmem(swapped(message_b, "gy", 1)))
    besides = [beside] + [moved(beside, "gx", step) for step in steps[1:]]
    operands = [in_vmem(value) for pair in zip(owns, besides) for value in pair]

    count = row_count // SUB
    scratch = [pltpu.SMEM(well_cells.shape, jnp.int32), pltpu.SMEM(well_rates.shape, f32), pltpu.SemaphoreType.DMA((3,))]
    whole = [pltpu.VMEM((LAYERS, width, blocks, count >> depth, SUB, LANES), f32) for depth, (width, _) in enumerate(LEVELS)]
    scratch += [whole[0], whole[0], whole[1], whole[2], whole[0]]
    scratch += [pltpu.VMEM((1,) + block, f32), pltpu.VMEM(block, f32)]
    for depth, (width, _) in enumerate(LEVELS):
        scratch += Level.scratch(count >> depth, width, blocks)
    state = jax.ShapeDtypeStruct((1, layer_count, row_count, col_count), f32)
    grid_shape = (layer_count, row_count * gx_count, col_count * gy_count)
    pressure, shuffled, terms = pl.pallas_call(
        partial(cycle_kernel, grid_shape, blocks),
        out_shape=[state, pltpu.VMEM((1,) + block, f32), pltpu.VMEM(block, f32)],
        in_specs=[hbm] * 2 + [vmem] * (2 * blocks),
        out_specs=[hbm, vmem, vmem],
        scratch_shapes=scratch,
        compiler_params=pltpu.CompilerParams(vmem_limit_bytes=24 * 1024 * 1024),
        name="cycles",
    )(in_hbm(well_cells), in_hbm(well_rates), *operands)
    gradient = summed(terms, "scen")
    adjoint = pl.pallas_call(
        order_kernel,
        out_shape=state,
        in_specs=[vmem],
        out_specs=vmem,
        cost_estimate=pl.CostEstimate(flops=2 * row_count * LANES**2 * 8, bytes_accessed=2**18, transcendentals=0),
        name="order",
    )(in_vmem(shuffled))
    return pressure, adjoint, gradient


def solution(mesh):
    return jax.shard_map(
        shards,
        mesh=mesh,
        in_specs=(
            P(None, "gx", "gy"),
            P(None, "gx", "gy"),
            P(),
            P(None, "gx", "gy"),
            P("scen", None, "gx", "gy"),
            P("scen", None, "gx", "gy"),
            P("scen", None),
            P("scen", None),
        ),
        out_specs=(P("scen", None, "gx", "gy"), P("scen", None, "gx", "gy"), P(None, "gx", "gy")),
        check_vma=False,
    )
```

profile of v0, /device:TPU:16, one launch (start us, length us, event | category | flops | bytes accessed | tf_op | source)
XLA Modules:
  0.0 24.2 jit_solution(4607313152673776025)
XLA Ops:
  0.6 1.5 %pack.1 = (f32[4,2,64,128]{3,2,1,0:T(8,128)S(1)}, f32[3,64,128]{2,1,0:T(8,128)S(1)}, f32[3,64,128]{2,1,0:T(8,128)S(1)}) custom-call(f32[4]{0:T(128)} %scale_hbm.1, f32[2,64,128]{2,1,0:T(8,128)} %perm_log_hbm.1, s32[2,64,128]{2,1,0:T(8,128)} %facies_hbm.1, f32[2,64,128]{2,1,0:T(8,128)} %acc_hbm.1, f32[1,2,64,128]{3,2,1,0:T(8,128)} %prev_hbm.1, ...), custom_call_target="tpu_custom_call" | custom-call | tf_op jit(solution)/shard_map/pack/pallas_call | solution.py:529
  2.1 1.6 %collective-permute-start = (f32[3,64,128]{2,1,0:T(8,128)S(1)}, f32[3,64,128]{2,1,0:T(8,128)S(1)}, u32[]{:S(2)}, u32[]{:S(2)}) collective-permute-start(f32[3,64,128]{2,1,0:T(8,128)S(1)} %get-tuple-element.10), channel_id=1, source_target_pairs={{0,1},{1,0},{2,3},{3,2},{4,5},{5,4},{6,7},{7,6},{8,9},{9,8},{10,11... | collective-permute-start | bytes 294920 | tf_op jit(solution)/shard_map/ppermute | solution.py:492
  3.8 1.9 %collective-permute-start.1 = (f32[3,64,128]{2,1,0:T(8,128)S(1)}, f32[3,64,128]{2,1,0:T(8,128)S(1)}, u32[]{:S(2)}, u32[]{:S(2)}) collective-permute-start(f32[3,64,128]{2,1,0:T(8,128)S(1)} %get-tuple-element.11), channel_id=1, source_target_pairs={{0,0},{1,2},{2,1},{3,3},{4,4},{5,6},{6,5},{7,7},{8,8},{9,10},{10,9... | collective-permute-start | bytes 294920 | tf_op jit(solution)/shard_map/ppermute | solution.py:492
  5.7 0.1 collective-permute-start.2
  5.8 1.0 %collective-permute-done.message_a = f32[3,64,128]{2,1,0:T(8,128)S(1)} collective-permute-done((f32[3,64,128]{2,1,0:T(8,128)S(1)}, f32[3,64,128]{2,1,0:T(8,128)S(1)}, u32[]{:S(2)}, u32[]{:S(2)}) %collective-permute-start) | collective-permute-done | bytes 98336 | tf_op jit(solution)/shard_map/ppermute | solution.py:492
  6.8 3.5 %collective-permute-done.1.message_b = f32[3,64,128]{2,1,0:T(8,128)S(1)} collective-permute-done((f32[3,64,128]{2,1,0:T(8,128)S(1)}, f32[3,64,128]{2,1,0:T(8,128)S(1)}, u32[]{:S(2)}, u32[]{:S(2)}) %collective-permute-start.1) | collective-permute-done | bytes 98336 | tf_op jit(solution)/shard_map/ppermute | solution.py:492
  10.3 0.2 merge.1.refs_3_
  10.5 0.1 collective-permute-start.3
  10.5 0.0 collective-permute-done.2.refs_4_
  10.6 1.5 %collective-permute-done.3.refs_5_ = f32[4,2,64,128]{3,2,1,0:T(8,128)S(1)} collective-permute-done((f32[4,2,64,128]{3,2,1,0:T(8,128)S(1)}, f32[4,2,64,128]{3,2,1,0:T(8,128)S(1)}, u32[]{:S(2)}, u32[]{:S(2)}) %collective-permute-start.3) | collective-permute-done | bytes 262176 | tf_op jit(solution)/shard_map/ppermute | solution.py:484
  12.1 4.2 %cycles.1 = (f32[1,2,64,128]{3,2,1,0:T(8,128)}, f32[1,2,64,128]{3,2,1,0:T(8,128)S(1)}, f32[2,64,128]{2,1,0:T(8,128)S(1)}) custom-call(s32[1,5]{1,0:T(1,128)} %refs_0_.1, f32[1,5]{1,0:T(1,128)} %refs_1_.1, f32[4,2,64,128]{3,2,1,0:T(8,128)S(1)} %get-tuple-element.9.refs_2_, f32[4,2,64,128]{3,2,1,0:T(8,128)S(1)} %merge.1.refs_3_, ...), custom_call_target="tpu_custom_call" | custom-call | tf_op jit(solution)/shard_map/cycles/pallas_call | solution.py:565
  16.3 2.5 %collective-permute-start.6 = (f32[2,64,128]{2,1,0:T(8,128)S(1)}, f32[2,64,128]{2,1,0:T(8,128)S(1)}, u32[]{:S(2)}, u32[]{:S(2)}) collective-permute-start(f32[2,64,128]{2,1,0:T(8,128)S(1)} %get-tuple-element.14), channel_id=1, source_target_pairs={{0,24},{8,16},{16,8},{24,0},{1,25},{9,17},{17,9},{25,1},{2,26},{10... | collective-permute-start | bytes 196616 | tf_op jit(solution)/shard_map/ppermute | solution.py:497
  18.8 0.5 %collective-permute-start.5 = (f32[2,64,128]{2,1,0:T(8,128)S(1)}, f32[2,64,128]{2,1,0:T(8,128)S(1)}, u32[]{:S(2)}, u32[]{:S(2)}) collective-permute-start(f32[2,64,128]{2,1,0:T(8,128)S(1)} %get-tuple-element.14), channel_id=1, source_target_pairs={{0,16},{8,24},{16,0},{24,8},{1,17},{9,25},{17,1},{25,9},{2,18},{10... | collective-permute-start | bytes 196616 | tf_op jit(solution)/shard_map/ppermute | solution.py:497
  19.3 0.5 %collective-permute-start.4 = (f32[2,64,128]{2,1,0:T(8,128)S(1)}, f32[2,64,128]{2,1,0:T(8,128)S(1)}, u32[]{:S(2)}, u32[]{:S(2)}) collective-permute-start(f32[2,64,128]{2,1,0:T(8,128)S(1)} %get-tuple-element.14), channel_id=1, source_target_pairs={{0,8},{8,0},{16,24},{24,16},{1,9},{9,1},{17,25},{25,17},{2,10},{10... | collective-permute-start | bytes 196616 | tf_op jit(solution)/shard_map/ppermute | solution.py:497
  19.9 0.8 %order.1 = f32[1,2,64,128]{3,2,1,0:T(8,128)} custom-call(f32[1,2,64,128]{3,2,1,0:T(8,128)S(1)} %get-tuple-element.13.shuffled), custom_call_target="tpu_custom_call" | custom-call | flops 16777216 | bytes 262144 | tf_op jit(solution)/shard_map/order/pallas_call | solution.py:575
  20.7 0.9 %collective-permute-done.6 = f32[2,64,128]{2,1,0:T(8,128)S(1)} collective-permute-done((f32[2,64,128]{2,1,0:T(8,128)S(1)}, f32[2,64,128]{2,1,0:T(8,128)S(1)}, u32[]{:S(2)}, u32[]{:S(2)}) %collective-permute-start.6) | collective-permute-done | bytes 65568 | tf_op jit(solution)/shard_map/ppermute | solution.py:497
  21.6 1.5 %collective-permute-done.5 = f32[2,64,128]{2,1,0:T(8,128)S(1)} collective-permute-done((f32[2,64,128]{2,1,0:T(8,128)S(1)}, f32[2,64,128]{2,1,0:T(8,128)S(1)}, u32[]{:S(2)}, u32[]{:S(2)}) %collective-permute-start.5) | collective-permute-done | bytes 65568 | tf_op jit(solution)/shard_map/ppermute | solution.py:497
  23.1 0.5 %collective-permute-done.4 = f32[2,64,128]{2,1,0:T(8,128)S(1)} collective-permute-done((f32[2,64,128]{2,1,0:T(8,128)S(1)}, f32[2,64,128]{2,1,0:T(8,128)S(1)}, u32[]{:S(2)}, u32[]{:S(2)}) %collective-permute-start.4) | collective-permute-done | bytes 65568 | tf_op jit(solution)/shard_map/ppermute | solution.py:497
  23.6 0.6 %add_add_fusion = f32[2,64,128]{2,1,0:T(8,128)} fusion(f32[2,64,128]{2,1,0:T(8,128)S(1)} %collective-permute-done.5, f32[2,64,128]{2,1,0:T(8,128)S(1)} %collective-permute-done.6, f32[2,64,128]{2,1,0:T(8,128)S(1)} %get-tuple-element.14, f32[2,64,128]{2,1,0:T(8,128)S(1)} %collective-permute-done.4), kind=kLoop, calls=%fused_computation | loop fusion | flops 49152 | bytes 327680 | tf_op jit(solution)/shard_map/add | solution.py:500
Async XLA Ops:
  2.1 4.7 %collective-permute-start = (f32[3,64,128]{2,1,0:T(8,128)S(1)}, f32[3,64,128]{2,1,0:T(8,128)S(1)}, u32[]{:S(2)}, u32[]{:S(2)}) collective-permute-start(f32[3,64,128]{2,1,0:T(8,128)S(1)} %get-tuple-element.10), channel_id=1, source_target_pairs={{0,1},{1,0},{2,3},{3,2},{4,5},{5,4},{6,7},{7,6},{8,9},{9,8},{10,11... | collective-permute-start | bytes 294920 | tf_op jit(solution)/shard_map/ppermute | solution.py:492
  3.8 6.5 %collective-permute-start.1 = (f32[3,64,128]{2,1,0:T(8,128)S(1)}, f32[3,64,128]{2,1,0:T(8,128)S(1)}, u32[]{:S(2)}, u32[]{:S(2)}) collective-permute-start(f32[3,64,128]{2,1,0:T(8,128)S(1)} %get-tuple-element.11), channel_id=1, source_target_pairs={{0,0},{1,2},{2,1},{3,3},{4,4},{5,6},{6,5},{7,7},{8,8},{9,10},{10,9... | collective-permute-start | bytes 294920 | tf_op jit(solution)/shard_map/ppermute | solution.py:492
  5.7 4.9 %collective-permute-start.2 = (f32[4,2,64,128]{3,2,1,0:T(8,128)S(1)}, f32[4,2,64,128]{3,2,1,0:T(8,128)S(1)}, u32[]{:S(2)}, u32[]{:S(2)}) collective-permute-start(f32[4,2,64,128]{3,2,1,0:T(8,128)S(1)} %get-tuple-element.9.refs_2_), channel_id=1, source_target_pairs={{4,0},{0,4},{5,1},{1,5},{6,2},{2,6},{7,3},{3,7},{12,8},{8,12},{13,... | collective-permute-start | bytes 786440 | tf_op jit(solution)/shard_map/ppermute | solution.py:484
  10.5 1.6 %collective-permute-start.3 = (f32[4,2,64,128]{3,2,1,0:T(8,128)S(1)}, f32[4,2,64,128]{3,2,1,0:T(8,128)S(1)}, u32[]{:S(2)}, u32[]{:S(2)}) collective-permute-start(f32[4,2,64,128]{3,2,1,0:T(8,128)S(1)} %merge.1.refs_3_), channel_id=1, source_target_pairs={{4,0},{0,4},{5,1},{1,5},{6,2},{2,6},{7,3},{3,7},{12,8},{8,12},{13,... | collective-permute-start | bytes 786440 | tf_op jit(solution)/shard_map/ppermute | solution.py:484
  16.3 5.3 %collective-permute-start.6 = (f32[2,64,128]{2,1,0:T(8,128)S(1)}, f32[2,64,128]{2,1,0:T(8,128)S(1)}, u32[]{:S(2)}, u32[]{:S(2)}) collective-permute-start(f32[2,64,128]{2,1,0:T(8,128)S(1)} %get-tuple-element.14), channel_id=1, source_target_pairs={{0,24},{8,16},{16,8},{24,0},{1,25},{9,17},{17,9},{25,1},{2,26},{10... | collective-permute-start | bytes 196616 | tf_op jit(solution)/shard_map/ppermute | solution.py:497
  18.8 4.3 %collective-permute-start.5 = (f32[2,64,128]{2,1,0:T(8,128)S(1)}, f32[2,64,128]{2,1,0:T(8,128)S(1)}, u32[]{:S(2)}, u32[]{:S(2)}) collective-permute-start(f32[2,64,128]{2,1,0:T(8,128)S(1)} %get-tuple-element.14), channel_id=1, source_target_pairs={{0,16},{8,24},{16,0},{24,8},{1,17},{9,25},{17,1},{25,9},{2,18},{10... | collective-permute-start | bytes 196616 | tf_op jit(solution)/shard_map/ppermute | solution.py:497
  19.3 4.3 %collective-permute-start.4 = (f32[2,64,128]{2,1,0:T(8,128)S(1)}, f32[2,64,128]{2,1,0:T(8,128)S(1)}, u32[]{:S(2)}, u32[]{:S(2)}) collective-permute-start(f32[2,64,128]{2,1,0:T(8,128)S(1)} %get-tuple-element.14), channel_id=1, source_target_pairs={{0,8},{8,0},{16,24},{24,16},{1,9},{9,1},{17,25},{25,17},{2,10},{10... | collective-permute-start | bytes 196616 | tf_op jit(solution)/shard_map/ppermute | solution.py:497
where the time goes:
time: 24.4 us; the launch traced here: 24.2 us
  waiting for transfers between devices  8.94 us (37%)
  starting transfers between devices  7.25 us (30%)
  Pallas kernels  6.72 us (28%)
  between operations  0.69 us (3%)
  other arithmetic  0.65 us (3%)
    ppermute x2, waiting for transfers between devices, swapped(): return lax.ppermute(value, axis, list(pairs.items()))  4.5 us
    pallas_call x1, Pallas kernels, shards(): pl.pallas_call(partial(cycle_kernel, grid_shape, blocks), out_shape=[stat...  4.24 us
    ppermute x3, starting transfers between devices, summed(): lax.ppermute(value, axis, [(i, i ^ step) for i in range(count)])  3.55 us
    ppermute x2, starting transfers between devices, swapped(): return lax.ppermute(value, axis, list(pairs.items()))  3.55 us
    ppermute x3, waiting for transfers between devices, summed(): lax.ppermute(value, axis, [(i, i ^ step) for i in range(count)])  2.93 us
    ppermute x2, waiting for transfers between devices, moved(): return lax.ppermute(value, axis, pairs)  1.51 us
    pallas_call x1, Pallas kernels, shards(): pl.pallas_call(pack_kernel, out_shape=[pltpu.VMEM((4,) + block, f32), plt...  1.48 us
    pallas_call x1, Pallas kernels, shards(): pl.pallas_call(order_kernel, out_shape=state, in_specs=[vmem], out_specs=...  0.8 us
  transfers between devices with their start and end apart: 7, of which 6 were waited for; matrix products, arithmetic and copies ran while one was open for 0% of the time, Pallas kernels for 4%

commit v1 on v0

--- a/solution.py
+++ b/solution.py
@@ -67,6 +67,19 @@
             ((place >= HALF // 2) & (place < HALF - NEAR), (place >= high) & (place < high + ROOM), -shift))
 
 
+def interleaved(rows):
+    count = rows.shape[0] // SUB
+    return jnp.concatenate([rows[pl.ds(t, SUB, stride=count), :] for t in range(count)], axis=0)
+
+
+def put_in_order(shuffled, ordered):
+    count = ordered.shape[-2] // SUB
+    natural = shuffle(shuffled, True)
+    for layer in range(LAYERS):
+        for t in range(count):
+            ordered[layer, pl.ds(t, SUB, stride=count), :] = natural[layer, t * SUB:(t + 1) * SUB]
+
+
 def pack_kernel(scale_hbm, perm_log_hbm, facies_hbm, acc_hbm, prev_hbm, obs_hbm, own, message_a, message_b,
                 scale, perm_log, facies, acc, prev, obs, sems):
     pairs = ((scale_hbm, scale), (perm_log_hbm, perm_log), (facies_hbm, facies), (acc_hbm, acc), (prev_hbm, prev),
@@ -76,11 +89,15 @@
         copy.start()
     for copy in copies:
         copy.wait()
-    label = facies[...]
+
+    def layers(ref):
+        return jnp.stack([interleaved(ref.at[layer]) for layer in range(LAYERS)])
+
+    label = layers(facies)
     factor = jnp.zeros(label.shape, jnp.float32)
     for number in range(FACIES):
         factor = factor + jnp.where(label == number, scale[number], jnp.float32(0.0))
-    fields = [shuffle(value, False) for value in (jnp.exp(perm_log[...]) * factor, acc[...], prev[0], obs[0])]
+    fields = [shuffle(value, False) for value in (jnp.exp(layers(perm_log)) * factor, layers(acc), layers(prev.at[0]), layers(obs.at[0]))]
     for number in range(4):
         own[number] = fields[number]
     place = place_in_half(label.shape)
@@ -101,8 +118,6 @@
 
 def merge_kernel(message_a, message_b, beside):
     place = place_in_half(beside.shape[2:])
-    gy, gy_count = lax.axis_index("gy"), lax.axis_size("gy")
-    inside = ((place < HALF // 2) & (gy < gy_count - 1)) | ((place >= HALF // 2) & (gy > 0))
     from_a = (place < HALF // 2) != (lax.axis_index("gy") % 2 == 1)
     full = [[], [], []]
     for plane in range(3):
@@ -111,7 +126,7 @@
         two = lane_roll(jnp.where(from_a, b, a), -(HALF // 2))
         for number, value in zip((0, 1) if plane < 2 else (2, 2), (one, two)):
             full[number].append(value)
-    near = ((place < NEAR) | (place >= HALF - NEAR)) & inside
+    near = (place < NEAR) | (place >= HALF - NEAR)
     for layer in range(LAYERS):
         observed = jnp.zeros(place.shape, jnp.float32)
         for number in range(3):
@@ -119,7 +134,7 @@
             beside[number, layer] = jnp.where(near, value, 0.0)
             for _, lanes, shift in spare_lanes(number, place):
                 observed = jnp.where(lanes, lane_roll(value, -shift), observed)
-        beside[OBS, layer] = jnp.where(inside, observed, 0.0)
+        beside[OBS, layer] = observed
 
 
 class Level:
@@ -376,7 +391,7 @@
 
 
 def order_kernel(shuffled, ordered):
-    ordered[...] = shuffle(shuffled[...], True)
+    put_in_order(shuffled[...], ordered.at[0])
 
 
 def cycle_kernel(grid_shape, blocks, *refs):
@@ -395,7 +410,7 @@
     finest, middle, bottom = levels
 
     def rows(t):
-        return pl.ds(t, SUB, stride=count)
+        return pl.ds(t * SUB, SUB)
 
     def fields(number, layer, b, t):
         low = lane_index() < HALF
@@ -462,18 +477,18 @@
                 pressure[key] = values[u]
                 finest.target[key] = values[u] - observed[u]
             if b == 0:
-                pressure_rows[0, layer, rows(t), :] = own_columns(*values)
-    pressure_rows[...] = shuffle(pressure_rows[...], True)
+                terms_rows[layer, rows(t), :] = own_columns(*values)
+    put_in_order(terms_rows[...], pressure_rows.at[0])
     pressure_copy = pltpu.make_async_copy(pressure_rows, pressure_out, sems.at[2])
     pressure_copy.start()
     vcycle(levels, True, 1)
     for t in range(count):
         for layer in range(LAYERS):
-            adjoint_out[0, layer, rows(t), :] = own_columns(*[finest.now[layer, u, 0, t] for u in range(2)])
+            adjoint_out[layer, rows(t), :] = own_columns(*[finest.now[layer, u, 0, t] for u in range(2)])
 
     for layer, t, terms in face_terms(finest, Field(finest, pressure), Field(finest, finest.now), perm):
         terms_rows[layer, rows(t), :] = terms
-    terms_out[...] = shuffle(terms_rows[...], True)
+    put_in_order(terms_rows[...], terms_out)
     pressure_copy.wait()
 
 
@@ -485,11 +500,10 @@
 
 
 def swapped(value, axis, first):
-    count = lax.axis_size(axis)
-    pairs = {i: i for i in range(count)}
-    for i in range(first, count - 1, 2):
-        pairs[i], pairs[i + 1] = i + 1, i
-    return lax.ppermute(value, axis, list(pairs.items()))
+    pairs = []
+    for i in range(first, lax.axis_size(axis) - 1, 2):
+        pairs += [(i, i + 1), (i + 1, i)]
+    return lax.ppermute(value, axis, pairs)
 
 
 def summed(value, axis):
@@ -564,7 +578,7 @@
     grid_shape = (layer_count, row_count * gx_count, col_count * gy_count)
     pressure, shuffled, terms = pl.pallas_call(
         partial(cycle_kernel, grid_shape, blocks),
-        out_shape=[state, pltpu.VMEM((1,) + block, f32), pltpu.VMEM(block, f32)],
+        out_shape=[state, pltpu.VMEM(block, f32), pltpu.VMEM(block, f32)],
         in_specs=[hbm] * 2 + [vmem] * (2 * blocks),
         out_specs=[hbm, vmem, vmem],
         scratch_shapes=scratch,

time: 24.4 us -> 24.4 us (level)
  no operation moved by 1% of the time
where the time goes in v1:
time: 24.4 us; the launch traced here: 24.2 us
  waiting for transfers between devices  8.94 us (37%)
  starting transfers between devices  7.25 us (30%)
  Pallas kernels  6.7 us (27%)
  between operations  0.69 us (3%)
  other arithmetic  0.65 us (3%)
    ppermute x2, waiting for transfers between devices, swapped(): return lax.ppermute(value, axis, pairs)  4.5 us
    pallas_call x1, Pallas kernels, shards(): pl.pallas_call(partial(cycle_kernel, grid_shape, blocks), out_shape=[stat...  4.22 us
    ppermute x3, starting transfers between devices, summed(): lax.ppermute(value, axis, [(i, i ^ step) for i in range(count)])  3.55 us
    ppermute x2, starting transfers between devices, swapped(): return lax.ppermute(value, axis, pairs)  3.55 us
    ppermute x3, waiting for transfers between devices, summed(): lax.ppermute(value, axis, [(i, i ^ step) for i in range(count)])  2.92 us
    ppermute x2, waiting for transfers between devices, moved(): return lax.ppermute(value, axis, pairs)  1.51 us
    pallas_call x1, Pallas kernels, shards(): pl.pallas_call(pack_kernel, out_shape=[pltpu.VMEM((4,) + block, f32), plt...  1.48 us
    pallas_call x1, Pallas kernels, shards(): pl.pallas_call(order_kernel, out_shape=state, in_specs=[vmem], out_specs=...  0.81 us
  transfers between devices with their start and end apart: 7, of which 6 were waited for; matrix products, arithmetic and copies ran while one was open for 0% of the time, Pallas kernels for 4%

profile of v1, /device:TPU:16, one launch (start us, length us, event | category | flops | bytes accessed | tf_op | source)
XLA Modules:
  0.0 24.2 jit_solution(4674496694706117900)
XLA Ops:
  0.6 1.5 %pack.1 = (f32[4,2,64,128]{3,2,1,0:T(8,128)S(1)}, f32[3,64,128]{2,1,0:T(8,128)S(1)}, f32[3,64,128]{2,1,0:T(8,128)S(1)}) custom-call(f32[4]{0:T(128)} %scale_hbm.1, f32[2,64,128]{2,1,0:T(8,128)} %perm_log_hbm.1, s32[2,64,128]{2,1,0:T(8,128)} %facies_hbm.1, f32[2,64,128]{2,1,0:T(8,128)} %acc_hbm.1, f32[1,2,64,128]{3,2,1,0:T(8,128)} %prev_hbm.1, ...), custom_call_target="tpu_custom_call" | custom-call | tf_op jit(solution)/shard_map/pack/pallas_call | solution.py:543
  2.1 1.6 %collective-permute-start = (f32[3,64,128]{2,1,0:T(8,128)S(1)}, f32[3,64,128]{2,1,0:T(8,128)S(1)}, u32[]{:S(2)}, u32[]{:S(2)}) collective-permute-start(f32[3,64,128]{2,1,0:T(8,128)S(1)} %get-tuple-element.10), channel_id=1, source_target_pairs={{0,1},{1,0},{2,3},{3,2},{4,5},{5,4},{6,7},{7,6},{8,9},{9,8},{10,11... | collective-permute-start | bytes 294920 | tf_op jit(solution)/shard_map/ppermute | solution.py:506
  3.8 1.9 %collective-permute-start.1 = (f32[3,64,128]{2,1,0:T(8,128)S(1)}, f32[3,64,128]{2,1,0:T(8,128)S(1)}, u32[]{:S(2)}, u32[]{:S(2)}) collective-permute-start(f32[3,64,128]{2,1,0:T(8,128)S(1)} %get-tuple-element.11), channel_id=1, source_target_pairs={{1,2},{2,1},{5,6},{6,5},{9,10},{10,9},{13,14},{14,13},{17,18},{18,... | collective-permute-start | bytes 294920 | tf_op jit(solution)/shard_map/ppermute | solution.py:506
  5.7 0.1 collective-permute-start.2
  5.8 1.0 %collective-permute-done.message_a = f32[3,64,128]{2,1,0:T(8,128)S(1)} collective-permute-done((f32[3,64,128]{2,1,0:T(8,128)S(1)}, f32[3,64,128]{2,1,0:T(8,128)S(1)}, u32[]{:S(2)}, u32[]{:S(2)}) %collective-permute-start) | collective-permute-done | bytes 98336 | tf_op jit(solution)/shard_map/ppermute | solution.py:506
  6.8 3.5 %collective-permute-done.1.message_b = f32[3,64,128]{2,1,0:T(8,128)S(1)} collective-permute-done((f32[3,64,128]{2,1,0:T(8,128)S(1)}, f32[3,64,128]{2,1,0:T(8,128)S(1)}, u32[]{:S(2)}, u32[]{:S(2)}) %collective-permute-start.1) | collective-permute-done | bytes 98336 | tf_op jit(solution)/shard_map/ppermute | solution.py:506
  10.3 0.2 merge.1.refs_3_
  10.5 0.1 collective-permute-start.3
  10.5 0.0 collective-permute-done.2.refs_4_
  10.6 1.5 %collective-permute-done.3.refs_5_ = f32[4,2,64,128]{3,2,1,0:T(8,128)S(1)} collective-permute-done((f32[4,2,64,128]{3,2,1,0:T(8,128)S(1)}, f32[4,2,64,128]{3,2,1,0:T(8,128)S(1)}, u32[]{:S(2)}, u32[]{:S(2)}) %collective-permute-start.3) | collective-permute-done | bytes 262176 | tf_op jit(solution)/shard_map/ppermute | solution.py:499
  12.1 4.2 %cycles.1 = (f32[1,2,64,128]{3,2,1,0:T(8,128)}, f32[2,64,128]{2,1,0:T(8,128)S(1)}, f32[2,64,128]{2,1,0:T(8,128)S(1)}) custom-call(s32[1,5]{1,0:T(1,128)} %refs_0_.1, f32[1,5]{1,0:T(1,128)} %refs_1_.1, f32[4,2,64,128]{3,2,1,0:T(8,128)S(1)} %get-tuple-element.9.refs_2_, f32[4,2,64,128]{3,2,1,0:T(8,128)S(1)} %merge.1.refs_3_, ...), custom_call_target="tpu_custom_call" | custom-call | tf_op jit(solution)/shard_map/cycles/pallas_call | solution.py:579
  16.3 2.5 %collective-permute-start.6 = (f32[2,64,128]{2,1,0:T(8,128)S(1)}, f32[2,64,128]{2,1,0:T(8,128)S(1)}, u32[]{:S(2)}, u32[]{:S(2)}) collective-permute-start(f32[2,64,128]{2,1,0:T(8,128)S(1)} %get-tuple-element.14), channel_id=1, source_target_pairs={{0,24},{8,16},{16,8},{24,0},{1,25},{9,17},{17,9},{25,1},{2,26},{10... | collective-permute-start | bytes 196616 | tf_op jit(solution)/shard_map/ppermute | solution.py:511
  18.8 0.5 %collective-permute-start.5 = (f32[2,64,128]{2,1,0:T(8,128)S(1)}, f32[2,64,128]{2,1,0:T(8,128)S(1)}, u32[]{:S(2)}, u32[]{:S(2)}) collective-permute-start(f32[2,64,128]{2,1,0:T(8,128)S(1)} %get-tuple-element.14), channel_id=1, source_target_pairs={{0,16},{8,24},{16,0},{24,8},{1,17},{9,25},{17,1},{25,9},{2,18},{10... | collective-permute-start | bytes 196616 | tf_op jit(solution)/shard_map/ppermute | solution.py:511
  19.3 0.5 %collective-permute-start.4 = (f32[2,64,128]{2,1,0:T(8,128)S(1)}, f32[2,64,128]{2,1,0:T(8,128)S(1)}, u32[]{:S(2)}, u32[]{:S(2)}) collective-permute-start(f32[2,64,128]{2,1,0:T(8,128)S(1)} %get-tuple-element.14), channel_id=1, source_target_pairs={{0,8},{8,0},{16,24},{24,16},{1,9},{9,1},{17,25},{25,17},{2,10},{10... | collective-permute-start | bytes 196616 | tf_op jit(solution)/shard_map/ppermute | solution.py:511
  19.8 0.8 %order.1 = f32[1,2,64,128]{3,2,1,0:T(8,128)} custom-call(f32[2,64,128]{2,1,0:T(8,128)S(1)} %get-tuple-element.13.shuffled), custom_call_target="tpu_custom_call" | custom-call | flops 16777216 | bytes 262144 | tf_op jit(solution)/shard_map/order/pallas_call | solution.py:589
  20.7 0.9 %collective-permute-done.6 = f32[2,64,128]{2,1,0:T(8,128)S(1)} collective-permute-done((f32[2,64,128]{2,1,0:T(8,128)S(1)}, f32[2,64,128]{2,1,0:T(8,128)S(1)}, u32[]{:S(2)}, u32[]{:S(2)}) %collective-permute-start.6) | collective-permute-done | bytes 65568 | tf_op jit(solution)/shard_map/ppermute | solution.py:511
  21.6 1.5 %collective-permute-done.5 = f32[2,64,128]{2,1,0:T(8,128)S(1)} collective-permute-done((f32[2,64,128]{2,1,0:T(8,128)S(1)}, f32[2,64,128]{2,1,0:T(8,128)S(1)}, u32[]{:S(2)}, u32[]{:S(2)}) %collective-permute-start.5) | collective-permute-done | bytes 65568 | tf_op jit(solution)/shard_map/ppermute | solution.py:511
  23.1 0.5 %collective-permute-done.4 = f32[2,64,128]{2,1,0:T(8,128)S(1)} collective-permute-done((f32[2,64,128]{2,1,0:T(8,128)S(1)}, f32[2,64,128]{2,1,0:T(8,128)S(1)}, u32[]{:S(2)}, u32[]{:S(2)}) %collective-permute-start.4) | collective-permute-done | bytes 65568 | tf_op jit(solution)/shard_map/ppermute | solution.py:511
  23.6 0.6 %add_add_fusion = f32[2,64,128]{2,1,0:T(8,128)} fusion(f32[2,64,128]{2,1,0:T(8,128)S(1)} %collective-permute-done.5, f32[2,64,128]{2,1,0:T(8,128)S(1)} %collective-permute-done.6, f32[2,64,128]{2,1,0:T(8,128)S(1)} %get-tuple-element.14, f32[2,64,128]{2,1,0:T(8,128)S(1)} %collective-permute-done.4), kind=kLoop, calls=%fused_computation | loop fusion | flops 49152 | bytes 327680 | tf_op jit(solution)/shard_map/add | solution.py:514
Async XLA Ops:
  2.1 4.7 %collective-permute-start = (f32[3,64,128]{2,1,0:T(8,128)S(1)}, f32[3,64,128]{2,1,0:T(8,128)S(1)}, u32[]{:S(2)}, u32[]{:S(2)}) collective-permute-start(f32[3,64,128]{2,1,0:T(8,128)S(1)} %get-tuple-element.10), channel_id=1, source_target_pairs={{0,1},{1,0},{2,3},{3,2},{4,5},{5,4},{6,7},{7,6},{8,9},{9,8},{10,11... | collective-permute-start | bytes 294920 | tf_op jit(solution)/shard_map/ppermute | solution.py:506
  3.8 6.5 %collective-permute-start.1 = (f32[3,64,128]{2,1,0:T(8,128)S(1)}, f32[3,64,128]{2,1,0:T(8,128)S(1)}, u32[]{:S(2)}, u32[]{:S(2)}) collective-permute-start(f32[3,64,128]{2,1,0:T(8,128)S(1)} %get-tuple-element.11), channel_id=1, source_target_pairs={{1,2},{2,1},{5,6},{6,5},{9,10},{10,9},{13,14},{14,13},{17,18},{18,... | collective-permute-start | bytes 294920 | tf_op jit(solution)/shard_map/ppermute | solution.py:506
  5.7 4.9 %collective-permute-start.2 = (f32[4,2,64,128]{3,2,1,0:T(8,128)S(1)}, f32[4,2,64,128]{3,2,1,0:T(8,128)S(1)}, u32[]{:S(2)}, u32[]{:S(2)}) collective-permute-start(f32[4,2,64,128]{3,2,1,0:T(8,128)S(1)} %get-tuple-element.9.refs_2_), channel_id=1, source_target_pairs={{4,0},{0,4},{5,1},{1,5},{6,2},{2,6},{7,3},{3,7},{12,8},{8,12},{13,... | collective-permute-start | bytes 786440 | tf_op jit(solution)/shard_map/ppermute | solution.py:499
  10.5 1.6 %collective-permute-start.3 = (f32[4,2,64,128]{3,2,1,0:T(8,128)S(1)}, f32[4,2,64,128]{3,2,1,0:T(8,128)S(1)}, u32[]{:S(2)}, u32[]{:S(2)}) collective-permute-start(f32[4,2,64,128]{3,2,1,0:T(8,128)S(1)} %merge.1.refs_3_), channel_id=1, source_target_pairs={{4,0},{0,4},{5,1},{1,5},{6,2},{2,6},{7,3},{3,7},{12,8},{8,12},{13,... | collective-permute-start | bytes 786440 | tf_op jit(solution)/shard_map/ppermute | solution.py:499
  16.3 5.3 %collective-permute-start.6 = (f32[2,64,128]{2,1,0:T(8,128)S(1)}, f32[2,64,128]{2,1,0:T(8,128)S(1)}, u32[]{:S(2)}, u32[]{:S(2)}) collective-permute-start(f32[2,64,128]{2,1,0:T(8,128)S(1)} %get-tuple-element.14), channel_id=1, source_target_pairs={{0,24},{8,16},{16,8},{24,0},{1,25},{9,17},{17,9},{25,1},{2,26},{10... | collective-permute-start | bytes 196616 | tf_op jit(solution)/shard_map/ppermute | solution.py:511
  18.8 4.3 %collective-permute-start.5 = (f32[2,64,128]{2,1,0:T(8,128)S(1)}, f32[2,64,128]{2,1,0:T(8,128)S(1)}, u32[]{:S(2)}, u32[]{:S(2)}) collective-permute-start(f32[2,64,128]{2,1,0:T(8,128)S(1)} %get-tuple-element.14), channel_id=1, source_target_pairs={{0,16},{8,24},{16,0},{24,8},{1,17},{9,25},{17,1},{25,9},{2,18},{10... | collective-permute-start | bytes 196616 | tf_op jit(solution)/shard_map/ppermute | solution.py:511
  19.3 4.3 %collective-permute-start.4 = (f32[2,64,128]{2,1,0:T(8,128)S(1)}, f32[2,64,128]{2,1,0:T(8,128)S(1)}, u32[]{:S(2)}, u32[]{:S(2)}) collective-permute-start(f32[2,64,128]{2,1,0:T(8,128)S(1)} %get-tuple-element.14), channel_id=1, source_target_pairs={{0,8},{8,0},{16,24},{24,16},{1,9},{9,1},{17,25},{25,17},{2,10},{10... | collective-permute-start | bytes 196616 | tf_op jit(solution)/shard_map/ppermute | solution.py:511

commit v2 on v1

--- a/solution.py
+++ b/solution.py
@@ -137,6 +137,35 @@
         beside[OBS, layer] = observed
 
 
+class State:
+    def __init__(self, ref, level):
+        self.ref = ref
+        self.level = level
+
+    def place(self, key):
+        layer, u, b, t = key
+        count = self.level.count
+        return layer, u, pl.ds(SUB + b * SUB * count + t, SUB, stride=count)
+
+    def __getitem__(self, key):
+        layer, u, rows = self.place(key)
+        return self.ref[layer, u, rows, :]
+
+    def __setitem__(self, key, value):
+        layer, u, rows = self.place(key)
+        self.ref[layer, u, rows, :] = value
+
+    def wrap(self):
+        rows = SUB * self.level.count * self.level.blocks
+        for layer, u in self.level.members():
+            self.ref[layer, u, SUB - 1:SUB, :] = self.ref[layer, u, SUB + rows - 1:SUB + rows, :]
+            self.ref[layer, u, SUB + rows:SUB + rows + 1, :] = self.ref[layer, u, SUB:SUB + 1, :]
+
+    @staticmethod
+    def scratch(count, width, blocks):
+        return pltpu.VMEM((LAYERS, width, SUB * (count * blocks + 2), LANES), jnp.float32)
+
+
 class Level:
     def __init__(self, count, width, span, blocks, refs):
         self.count = count
@@ -144,7 +173,8 @@
         self.span = span
         self.blocks = blocks
         (self.c_south, self.c_first, self.c_inner, self.c_east, self.c_west, self.c_layer, self.weight, self.diag,
-         self.target, self.now, self.later) = refs
+         self.target, now, later) = refs
+        self.now, self.later = State(now, self), State(later, self)
 
     @staticmethod
     def scratch(count, width, blocks):
@@ -153,7 +183,8 @@
 
         whole = vectors(LAYERS, width, blocks, count)
         edge = vectors(LAYERS, blocks, count)
-        return [whole, vectors(LAYERS, width, blocks), edge, edge, edge, vectors(width, blocks, count)] + [whole] * 5
+        return [whole, vectors(LAYERS, width, blocks), edge, edge, edge, vectors(width, blocks, count)] + [whole] * 3 + [
+            State.scratch(count, width, blocks)] * 2
 
     def steps(self, ring=None):
         for b in range(self.blocks):
@@ -173,38 +204,17 @@
     return [jnp.where(edge, rolled[b - 1], rolled[b]) for b in range(len(values))]
 
 
-def row_after(values):
-    edge = row_index() >= SUB - 1
-    rolled = [row_roll(value, -1) for value in values]
-    return [jnp.where(edge, rolled[(b + 1) % len(values)], rolled[b]) for b in range(len(values))]
-
-
 class Field:
-    def __init__(self, level, source, coarse=None):
+    def __init__(self, source, coarse=None):
         self.source = source
         self.coarse = coarse
-        self.count = level.count
         self.read = {}
-        self.before, self.after = {}, {}
-        for layer, u in level.members():
-            lows = row_before([self.value(layer, u, b, level.count - 1) for b in range(level.blocks)])
-            highs = row_after([self.value(layer, u, b, 0) for b in range(level.blocks)])
-            for b in range(level.blocks):
-                self.before[layer, u, b] = lows[b]
-                self.after[layer, u, b] = highs[b]
-
-    def value(self, layer, u, b, t):
-        value = self.source[layer, u, b, t]
-        return value if self.coarse is None else value + self.coarse[layer, 0, b, t // 2]
 
     def at(self, layer, u, b, t):
-        if t < 0:
-            return self.before[layer, u, b]
-        if t >= self.count:
-            return self.after[layer, u, b]
         key = layer, u, b, t
         if key not in self.read:
-            self.read[key] = self.value(*key)
+            value = self.source[key]
+            self.read[key] = value if self.coarse is None else value + self.coarse[layer, 0, b, t // 2]
         return self.read[key]
 
 
@@ -213,7 +223,7 @@
 
 
 def neighbour_sums(level, source, ring=None, coarse=None):
-    field = Field(level, source, coarse)
+    field = Field(source, coarse)
     coeffs = {}
     for b, t in level.steps(ring):
         for member in level.members():
@@ -240,6 +250,7 @@
 def sweep(level, source, result, ring=None, coarse=None):
     for key, value, total in neighbour_sums(level, source, ring, coarse):
         result[key] = (1.0 - damping) * value + level.weight[key] * (level.target[key] + total)
+    result.wrap()
 
 
 def sweeps(level, count, ring=None, coarse=None):
@@ -254,6 +265,7 @@
         for layer, u in level.members():
             key = layer, u, b, t
             level.now[key] = level.weight[key] * level.target[key]
+    level.now.wrap()
 
 
 def pair_sum(value, span):
@@ -408,6 +420,7 @@
     levels = [Level(count >> depth, width, span, blocks, refs[11 * depth:11 * depth + 11])
               for depth, (width, span) in enumerate(LEVELS)]
     finest, middle, bottom = levels
+    pressure = State(pressure, finest)
 
     def rows(t):
         return pl.ds(t * SUB, SUB)
@@ -434,6 +447,7 @@
                 acc[key] = accs[u]
                 finest.now[key] = starts[u]
                 finest.target[key] = accs[u] * starts[u]
+    finest.now.wrap()
 
     for copy in copies:
         copy.wait()
@@ -478,6 +492,7 @@
                 finest.target[key] = values[u] - observed[u]
             if b == 0:
                 terms_rows[layer, rows(t), :] = own_columns(*values)
+    pressure.wrap()
     put_in_order(terms_rows[...], pressure_rows.at[0])
     pressure_copy = pltpu.make_async_copy(pressure_rows, pressure_out, sems.at[2])
     pressure_copy.start()
@@ -486,7 +501,7 @@
         for layer in range(LAYERS):
             adjoint_out[layer, rows(t), :] = own_columns(*[finest.now[layer, u, 0, t] for u in range(2)])
 
-    for layer, t, terms in face_terms(finest, Field(finest, pressure), Field(finest, finest.now), perm):
+    for layer, t, terms in face_terms(finest, Field(pressure), Field(finest.now), perm):
         terms_rows[layer, rows(t), :] = terms
     put_in_order(terms_rows[...], terms_out)
     pressure_copy.wait()
@@ -570,7 +585,7 @@
     count = row_count // SUB
     scratch = [pltpu.SMEM(well_cells.shape, jnp.int32), pltpu.SMEM(well_rates.shape, f32), pltpu.SemaphoreType.DMA((3,))]
     whole = [pltpu.VMEM((LAYERS, width, blocks, count >> depth, SUB, LANES), f32) for depth, (width, _) in enumerate(LEVELS)]
-    scratch += [whole[0], whole[0], whole[1], whole[2], whole[0]]
+    scratch += [whole[0], whole[0], whole[1], whole[2], State.scratch(count, LEVELS[0][0], blocks)]
     scratch += [pltpu.VMEM((1,) + block, f32), pltpu.VMEM(block, f32)]
     for depth, (width, _) in enumerate(LEVELS):
         scratch += Level.scratch(count >> depth, width, blocks)

time: 24.4 us -> 25.1 us (1.029)
  Pallas kernels: 6.7 us -> 7.42 us
    pallas_call x1, Pallas kernels: 4.22 us -> 4.93 us  [shards(): pl.pallas_call(partial(cycle_kernel, grid_shape, blocks), out_shape=[stat...]
where the time goes in v2:
time: 25.1 us; the launch traced here: 24.9 us
  waiting for transfers between devices  8.94 us (36%)
  Pallas kernels  7.42 us (30%)
  starting transfers between devices  7.25 us (29%)
  between operations  0.69 us (3%)
  other arithmetic  0.65 us (3%)
    pallas_call x1, Pallas kernels, shards(): pl.pallas_call(partial(cycle_kernel, grid_shape, blocks), out_shape=[stat...  4.93 us
    ppermute x2, waiting for transfers between devices, swapped(): return lax.ppermute(value, axis, pairs)  4.5 us
    ppermute x3, starting transfers between devices, summed(): lax.ppermute(value, axis, [(i, i ^ step) for i in range(count)])  3.55 us
    ppermute x2, starting transfers between devices, swapped(): return lax.ppermute(value, axis, pairs)  3.55 us
    ppermute x3, waiting for transfers between devices, summed(): lax.ppermute(value, axis, [(i, i ^ step) for i in range(count)])  2.92 us
    ppermute x2, waiting for transfers between devices, moved(): return lax.ppermute(value, axis, pairs)  1.51 us
    pallas_call x1, Pallas kernels, shards(): pl.pallas_call(pack_kernel, out_shape=[pltpu.VMEM((4,) + block, f32), plt...  1.48 us
    pallas_call x1, Pallas kernels, shards(): pl.pallas_call(order_kernel, out_shape=state, in_specs=[vmem], out_specs=...  0.81 us
  transfers between devices with their start and end apart: 7, of which 6 were waited for; matrix products, arithmetic and copies ran while one was open for 0% of the time, Pallas kernels for 4%

profile of v2, /device:TPU:16, one launch (start us, length us, event | category | flops | bytes accessed | tf_op | source)
XLA Modules:
  0.0 24.9 jit_solution(3065727879475742904)
XLA Ops:
  0.6 1.5 %pack.1 = (f32[4,2,64,128]{3,2,1,0:T(8,128)S(1)}, f32[3,64,128]{2,1,0:T(8,128)S(1)}, f32[3,64,128]{2,1,0:T(8,128)S(1)}) custom-call(f32[4]{0:T(128)} %scale_hbm.1, f32[2,64,128]{2,1,0:T(8,128)} %perm_log_hbm.1, s32[2,64,128]{2,1,0:T(8,128)} %facies_hbm.1, f32[2,64,128]{2,1,0:T(8,128)} %acc_hbm.1, f32[1,2,64,128]{3,2,1,0:T(8,128)} %prev_hbm.1, ...), custom_call_target="tpu_custom_call" | custom-call | tf_op jit(solution)/shard_map/pack/pallas_call | solution.py:558
  2.1 1.6 %collective-permute-start = (f32[3,64,128]{2,1,0:T(8,128)S(1)}, f32[3,64,128]{2,1,0:T(8,128)S(1)}, u32[]{:S(2)}, u32[]{:S(2)}) collective-permute-start(f32[3,64,128]{2,1,0:T(8,128)S(1)} %get-tuple-element.10), channel_id=1, source_target_pairs={{0,1},{1,0},{2,3},{3,2},{4,5},{5,4},{6,7},{7,6},{8,9},{9,8},{10,11... | collective-permute-start | bytes 294920 | tf_op jit(solution)/shard_map/ppermute | solution.py:521
  3.8 1.9 %collective-permute-start.1 = (f32[3,64,128]{2,1,0:T(8,128)S(1)}, f32[3,64,128]{2,1,0:T(8,128)S(1)}, u32[]{:S(2)}, u32[]{:S(2)}) collective-permute-start(f32[3,64,128]{2,1,0:T(8,128)S(1)} %get-tuple-element.11), channel_id=1, source_target_pairs={{1,2},{2,1},{5,6},{6,5},{9,10},{10,9},{13,14},{14,13},{17,18},{18,... | collective-permute-start | bytes 294920 | tf_op jit(solution)/shard_map/ppermute | solution.py:521
  5.7 0.1 collective-permute-start.2
  5.8 1.0 %collective-permute-done.message_a = f32[3,64,128]{2,1,0:T(8,128)S(1)} collective-permute-done((f32[3,64,128]{2,1,0:T(8,128)S(1)}, f32[3,64,128]{2,1,0:T(8,128)S(1)}, u32[]{:S(2)}, u32[]{:S(2)}) %collective-permute-start) | collective-permute-done | bytes 98336 | tf_op jit(solution)/shard_map/ppermute | solution.py:521
  6.8 3.5 %collective-permute-done.1.message_b = f32[3,64,128]{2,1,0:T(8,128)S(1)} collective-permute-done((f32[3,64,128]{2,1,0:T(8,128)S(1)}, f32[3,64,128]{2,1,0:T(8,128)S(1)}, u32[]{:S(2)}, u32[]{:S(2)}) %collective-permute-start.1) | collective-permute-done | bytes 98336 | tf_op jit(solution)/shard_map/ppermute | solution.py:521
  10.3 0.2 merge.1.refs_3_
  10.5 0.1 collective-permute-start.3
  10.5 0.0 collective-permute-done.2.refs_4_
  10.6 1.5 %collective-permute-done.3.refs_5_ = f32[4,2,64,128]{3,2,1,0:T(8,128)S(1)} collective-permute-done((f32[4,2,64,128]{3,2,1,0:T(8,128)S(1)}, f32[4,2,64,128]{3,2,1,0:T(8,128)S(1)}, u32[]{:S(2)}, u32[]{:S(2)}) %collective-permute-start.3) | collective-permute-done | bytes 262176 | tf_op jit(solution)/shard_map/ppermute | solution.py:514
  12.1 4.9 %cycles.1 = (f32[1,2,64,128]{3,2,1,0:T(8,128)}, f32[2,64,128]{2,1,0:T(8,128)S(1)}, f32[2,64,128]{2,1,0:T(8,128)S(1)}) custom-call(s32[1,5]{1,0:T(1,128)} %refs_0_.1, f32[1,5]{1,0:T(1,128)} %refs_1_.1, f32[4,2,64,128]{3,2,1,0:T(8,128)S(1)} %get-tuple-element.9.refs_2_, f32[4,2,64,128]{3,2,1,0:T(8,128)S(1)} %merge.1.refs_3_, ...), custom_call_target="tpu_custom_call" | custom-call | tf_op jit(solution)/shard_map/cycles/pallas_call | solution.py:594
  17.0 2.5 %collective-permute-start.6 = (f32[2,64,128]{2,1,0:T(8,128)S(1)}, f32[2,64,128]{2,1,0:T(8,128)S(1)}, u32[]{:S(2)}, u32[]{:S(2)}) collective-permute-start(f32[2,64,128]{2,1,0:T(8,128)S(1)} %get-tuple-element.14), channel_id=1, source_target_pairs={{0,24},{8,16},{16,8},{24,0},{1,25},{9,17},{17,9},{25,1},{2,26},{10... | collective-permute-start | bytes 196616 | tf_op jit(solution)/shard_map/ppermute | solution.py:526
  19.5 0.5 %collective-permute-start.5 = (f32[2,64,128]{2,1,0:T(8,128)S(1)}, f32[2,64,128]{2,1,0:T(8,128)S(1)}, u32[]{:S(2)}, u32[]{:S(2)}) collective-permute-start(f32[2,64,128]{2,1,0:T(8,128)S(1)} %get-tuple-element.14), channel_id=1, source_target_pairs={{0,16},{8,24},{16,0},{24,8},{1,17},{9,25},{17,1},{25,9},{2,18},{10... | collective-permute-start | bytes 196616 | tf_op jit(solution)/shard_map/ppermute | solution.py:526
  20.0 0.5 %collective-permute-start.4 = (f32[2,64,128]{2,1,0:T(8,128)S(1)}, f32[2,64,128]{2,1,0:T(8,128)S(1)}, u32[]{:S(2)}, u32[]{:S(2)}) collective-permute-start(f32[2,64,128]{2,1,0:T(8,128)S(1)} %get-tuple-element.14), channel_id=1, source_target_pairs={{0,8},{8,0},{16,24},{24,16},{1,9},{9,1},{17,25},{25,17},{2,10},{10... | collective-permute-start | bytes 196616 | tf_op jit(solution)/shard_map/ppermute | solution.py:526
  20.6 0.8 %order.1 = f32[1,2,64,128]{3,2,1,0:T(8,128)} custom-call(f32[2,64,128]{2,1,0:T(8,128)S(1)} %get-tuple-element.13.shuffled), custom_call_target="tpu_custom_call" | custom-call | flops 16777216 | bytes 262144 | tf_op jit(solution)/shard_map/order/pallas_call | solution.py:604
  21.4 0.9 %collective-permute-done.6 = f32[2,64,128]{2,1,0:T(8,128)S(1)} collective-permute-done((f32[2,64,128]{2,1,0:T(8,128)S(1)}, f32[2,64,128]{2,1,0:T(8,128)S(1)}, u32[]{:S(2)}, u32[]{:S(2)}) %collective-permute-start.6) | collective-permute-done | bytes 65568 | tf_op jit(solution)/shard_map/ppermute | solution.py:526
  22.3 1.5 %collective-permute-done.5 = f32[2,64,128]{2,1,0:T(8,128)S(1)} collective-permute-done((f32[2,64,128]{2,1,0:T(8,128)S(1)}, f32[2,64,128]{2,1,0:T(8,128)S(1)}, u32[]{:S(2)}, u32[]{:S(2)}) %collective-permute-start.5) | collective-permute-done | bytes 65568 | tf_op jit(solution)/shard_map/ppermute | solution.py:526
  23.8 0.5 %collective-permute-done.4 = f32[2,64,128]{2,1,0:T(8,128)S(1)} collective-permute-done((f32[2,64,128]{2,1,0:T(8,128)S(1)}, f32[2,64,128]{2,1,0:T(8,128)S(1)}, u32[]{:S(2)}, u32[]{:S(2)}) %collective-permute-start.4) | collective-permute-done | bytes 65568 | tf_op jit(solution)/shard_map/ppermute | solution.py:526
  24.3 0.6 %add_add_fusion = f32[2,64,128]{2,1,0:T(8,128)} fusion(f32[2,64,128]{2,1,0:T(8,128)S(1)} %collective-permute-done.5, f32[2,64,128]{2,1,0:T(8,128)S(1)} %collective-permute-done.6, f32[2,64,128]{2,1,0:T(8,128)S(1)} %get-tuple-element.14, f32[2,64,128]{2,1,0:T(8,128)S(1)} %collective-permute-done.4), kind=kLoop, calls=%fused_computation | loop fusion | flops 49152 | bytes 327680 | tf_op jit(solution)/shard_map/add | solution.py:529
Async XLA Ops:
  2.1 4.7 %collective-permute-start = (f32[3,64,128]{2,1,0:T(8,128)S(1)}, f32[3,64,128]{2,1,0:T(8,128)S(1)}, u32[]{:S(2)}, u32[]{:S(2)}) collective-permute-start(f32[3,64,128]{2,1,0:T(8,128)S(1)} %get-tuple-element.10), channel_id=1, source_target_pairs={{0,1},{1,0},{2,3},{3,2},{4,5},{5,4},{6,7},{7,6},{8,9},{9,8},{10,11... | collective-permute-start | bytes 294920 | tf_op jit(solution)/shard_map/ppermute | solution.py:521
  3.8 6.5 %collective-permute-start.1 = (f32[3,64,128]{2,1,0:T(8,128)S(1)}, f32[3,64,128]{2,1,0:T(8,128)S(1)}, u32[]{:S(2)}, u32[]{:S(2)}) collective-permute-start(f32[3,64,128]{2,1,0:T(8,128)S(1)} %get-tuple-element.11), channel_id=1, source_target_pairs={{1,2},{2,1},{5,6},{6,5},{9,10},{10,9},{13,14},{14,13},{17,18},{18,... | collective-permute-start | bytes 294920 | tf_op jit(solution)/shard_map/ppermute | solution.py:521
  5.7 4.9 %collective-permute-start.2 = (f32[4,2,64,128]{3,2,1,0:T(8,128)S(1)}, f32[4,2,64,128]{3,2,1,0:T(8,128)S(1)}, u32[]{:S(2)}, u32[]{:S(2)}) collective-permute-start(f32[4,2,64,128]{3,2,1,0:T(8,128)S(1)} %get-tuple-element.9.refs_2_), channel_id=1, source_target_pairs={{4,0},{0,4},{5,1},{1,5},{6,2},{2,6},{7,3},{3,7},{12,8},{8,12},{13,... | collective-permute-start | bytes 786440 | tf_op jit(solution)/shard_map/ppermute | solution.py:514
  10.5 1.6 %collective-permute-start.3 = (f32[4,2,64,128]{3,2,1,0:T(8,128)S(1)}, f32[4,2,64,128]{3,2,1,0:T(8,128)S(1)}, u32[]{:S(2)}, u32[]{:S(2)}) collective-permute-start(f32[4,2,64,128]{3,2,1,0:T(8,128)S(1)} %merge.1.refs_3_), channel_id=1, source_target_pairs={{4,0},{0,4},{5,1},{1,5},{6,2},{2,6},{7,3},{3,7},{12,8},{8,12},{13,... | collective-permute-start | bytes 786440 | tf_op jit(solution)/shard_map/ppermute | solution.py:514
  17.0 5.3 %collective-permute-start.6 = (f32[2,64,128]{2,1,0:T(8,128)S(1)}, f32[2,64,128]{2,1,0:T(8,128)S(1)}, u32[]{:S(2)}, u32[]{:S(2)}) collective-permute-start(f32[2,64,128]{2,1,0:T(8,128)S(1)} %get-tuple-element.14), channel_id=1, source_target_pairs={{0,24},{8,16},{16,8},{24,0},{1,25},{9,17},{17,9},{25,1},{2,26},{10... | collective-permute-start | bytes 196616 | tf_op jit(solution)/shard_map/ppermute | solution.py:526
  19.5 4.3 %collective-permute-start.5 = (f32[2,64,128]{2,1,0:T(8,128)S(1)}, f32[2,64,128]{2,1,0:T(8,128)S(1)}, u32[]{:S(2)}, u32[]{:S(2)}) collective-permute-start(f32[2,64,128]{2,1,0:T(8,128)S(1)} %get-tuple-element.14), channel_id=1, source_target_pairs={{0,16},{8,24},{16,0},{24,8},{1,17},{9,25},{17,1},{25,9},{2,18},{10... | collective-permute-start | bytes 196616 | tf_op jit(solution)/shard_map/ppermute | solution.py:526
  20.0 4.3 %collective-permute-start.4 = (f32[2,64,128]{2,1,0:T(8,128)S(1)}, f32[2,64,128]{2,1,0:T(8,128)S(1)}, u32[]{:S(2)}, u32[]{:S(2)}) collective-permute-start(f32[2,64,128]{2,1,0:T(8,128)S(1)} %get-tuple-element.14), channel_id=1, source_target_pairs={{0,8},{8,0},{16,24},{24,16},{1,9},{9,1},{17,25},{25,17},{2,10},{10... | collective-permute-start | bytes 196616 | tf_op jit(solution)/shard_map/ppermute | solution.py:526
